TPU v7x, 512 devices: a whole 4x4x16 slice. The times are simulated.
512 devices in a mesh: replica: 32 (over z, y_lo), fsdp: 16 (over x, y_hi, core).
Axes of the slice: x: 4, y: 4 (y_hi: 2, y_lo: 2; y = y_hi * 2 + y_lo), z: 16, core: 2. Of those that a mesh axis runs over, the one named last changes fastest.
Arguments:
- tokens: bfloat16 [32, 2048, 4096], P('replica', 'fsdp'), may hold values from -6 to 6
- local_weight: bfloat16 [32, 4096, 512], P('replica', 'fsdp'), may hold values from -6 to 6
- key_cot: bfloat16 [32, 2048, 512], P('replica', 'fsdp'), may hold values from -6 to 6
- global_weight: float32 [4096, 512], P(('fsdp', 'replica')), may hold values from -6 to 6
- momentum: float32 [4096, 512], P(('fsdp', 'replica')), may hold values from -6 to 6
- anchor: float32 [4096, 512], P(('fsdp', 'replica')), may hold values from -6 to 6
Outputs:
- keys: bfloat16 [32, 2048, 512], P('replica', 'fsdp')
- grad_tokens: bfloat16 [32, 2048, 4096], P('replica', 'fsdp')
- grad_weight: bfloat16 [32, 4096, 512], P('replica', 'fsdp')
- momentum_new: float32 [4096, 512], P(('fsdp', 'replica'))
- global_new: float32 [4096, 512], P(('fsdp', 'replica'))
- synced: bfloat16 [4096, 512], P('fsdp')
All inputs are finite; a program needn't handle non-finite values.
Results may differ from a plain program's by a relative error of at most 0.0095.
Values may be sent and summed in bfloat16 or wider, within the bound.
A program may use at most 64 MiB of HBM per device.

v0:
```python
import jax
import jax.numpy as jnp
from jax import lax
from jax.sharding import PartitionSpec as P

D_WIN = 4096


def on_device(tokens, local_weight, key_cot, global_weight, momentum, anchor):
    scale = 1.0 / D_WIN**0.5
    inputs = tokens[0]
    weight = local_weight[0]
    cot = key_cot[0]
    total = lax.psum_scatter(
        weight.astype(jnp.float32).astype(jnp.bfloat16), "replica", scatter_dimension=0, tiled=True
    ).astype(jnp.float32)
    pseudo = global_weight - total / lax.axis_size("replica")
    push = pseudo + 0.1 * (global_weight - anchor)
    momentum_new = 0.9 * momentum + push
    global_new = global_weight - 0.7 * (push + 0.9 * momentum_new)
    synced = lax.all_gather(global_new.astype(jnp.bfloat16), "replica", axis=0, tiled=True)
    columns_all = lax.all_to_all(inputs, "fsdp", split_axis=1, concat_axis=0, tiled=True)
    cot_all = lax.all_gather(cot, "fsdp", axis=0, tiled=True)
    wgrad = lax.dot_general(
        columns_all, cot_all, (((0,), (0,)), ((), ())), preferred_element_type=jnp.float32
    )
    grad_weight = (wgrad * scale).astype(jnp.bfloat16)
    piece = lax.all_gather(weight, "fsdp", axis=0, tiled=True)
    key_total = jnp.dot(inputs, piece, preferred_element_type=jnp.float32)
    part = lax.dot_general(cot, piece, (((1,), (1,)), ((), ())), preferred_element_type=jnp.float32)
    back_full = part
    summed, back_full = (key_total, back_full)
    keys = (summed * scale).astype(jnp.bfloat16)
    grad_tokens = (back_full * scale).astype(jnp.bfloat16)
    return (keys[None], grad_tokens[None], grad_weight[None], momentum_new, global_new, synced)


def solution(mesh):
    in_specs = (
        P("replica", "fsdp", None),
        P("replica", "fsdp", None),
        P("replica", "fsdp", None),
        P(("fsdp", "replica"), None),
        P(("fsdp", "replica"), None),
        P(("fsdp", "replica"), None),
    )
    out_specs = (
        P("replica", "fsdp", None),
        P("replica", "fsdp", None),
        P("replica", "fsdp", None),
        P(("fsdp", "replica"), None),
        P(("fsdp", "replica"), None),
        P("fsdp", None),
    )
    return jax.shard_map(
        on_device, mesh=mesh, in_specs=in_specs, out_specs=out_specs, check_vma=False
    )
```

profile of v0, /device:TPU:16, one launch (start us, length us, event | category | flops | bytes accessed | tf_op | source)
XLA Modules:
  0.0 245.4 jit_solution(13214008306867970524)
XLA Ops:
  8.0 0.0 copy-start.3
  8.0 0.0 copy-start.4
  8.0 0.0 copy-start.5
  8.0 0.0 reduce-scatter.2.cloned.1.call-start
  8.1 0.7 reduce-scatter.2.cloned.1.call-update
  8.8 0.0 all-gather.7.cloned.1.call-start
  8.8 0.5 all-gather.7.cloned.1.call-update
  9.3 0.0 all-gather.5.cloned.1.call-start
  9.4 0.5 all-gather.5.cloned.1.call-update
  9.9 2.3 copy.12
  12.2 9.3 %all-to-all-start = ((bf16[128,16,256]{0,2,1:T(8,128)(2,1)}), bf16[128,16,256]{0,2,1:T(8,128)(2,1)S(1)}, u32[]{:S(2)}, u32[]{:S(2)}) async-start(bf16[128,16,256]{0,2,1:T(8,128)(2,1)} %bitcast.5), calls=%async_computation | async-start | bytes 2097152 | tf_op jit(solution)/shard_map/all_to_all | solution.py:22
  21.5 142.5 %reduce-scatter.2.cloned.1.call-done = bf16[8,512]{1,0:T(8,128)(2,1)} async-done(((bf16[256,512]{1,0:T(8,128)(2,1)}), bf16[8,512]{1,0:T(8,128)(2,1)}) %reduce-scatter.2.cloned.1.call-update) | async-done | bytes 8208 | tf_op jit(solution)/shard_map/reduce_scatter | solution.py:14
  164.0 0.0 copy-done.3
  164.0 1.3 fusion.27
  165.4 62.1 %all_gather.11 = bf16[256,512]{1,0:T(8,128)(2,1)S(1)} all-gather(bf16[8,512]{1,0:T(8,128)(2,1)S(1)} %get-tuple-element.6), channel_id=1, replica_groups=mesh['replica'=32,'fsdp'=16] {'replica'}, dimensions={0}, use_global_device_ids=true | all-gather | bytes 270336 | tf_op jit(solution)/shard_map/all_gather | solution.py:21
  227.4 0.0 all-to-all-done
  227.4 0.5 copy.13
  228.0 0.0 all-gather.7.cloned.1.call-done
  228.0 0.0 copy-start.2
  228.0 3.1 %fusion.13 = bf16[1,256,512]{2,1,0:T(8,128)(2,1)} fusion(bf16[2048,256]{1,0:T(8,128)(2,1)S(1)} %bitcast.38, bf16[1,2048,512]{2,1,0:T(8,128)(2,1)} %all-gather.7.cloned.1.call-done), kind=kOutput, calls=%fused_computation.10 | convolution fusion | flops 537133056 | bytes 3407872 | tf_op jit(solution)/shard_map/dot_general | solution.py:24
  231.1 3.7 %fusion.22 = bf16[1,128,512]{2,1,0:T(8,128)(2,1)} fusion(bf16[1,4096,512]{2,1,0:T(8,128)(2,1)} %all-gather.5.cloned.1.call-done, bf16[1,128,4096]{2,1,0:T(8,128)(2,1)S(1)} %copy-done.1), kind=kOutput, calls=%fused_computation.13 | convolution fusion | flops 537001984 | bytes 5373952 | tf_op jit(solution)/shard_map/dot_general | solution.py:29
  234.8 0.0 copy-done
  234.8 2.5 %fusion.1 = bf16[1,128,4096]{2,1,0:T(8,128)(2,1)} fusion(bf16[1,4096,512]{2,1,0:T(8,128)(2,1)S(1)} %copy-done, bf16[1,128,512]{2,1,0:T(8,128)(2,1)S(1)} %copy-done.2), kind=kOutput, calls=%fused_computation.2 | convolution fusion | flops 537919488 | bytes 5373952 | tf_op jit(solution)/shard_map/dot_general | solution.py:30
  237.2 0.7 copy.15
  (7 shorter events, 0.0 us)
Async XLA Ops:
  8.0 156.0 %copy-start.3 = (f32[8,512]{1,0:T(8,128)S(1)}, f32[8,512]{1,0:T(8,128)}, u32[]{:S(2)}) copy-start(f32[8,512]{1,0:T(8,128)} %param.9) | copy-start | bytes 49156
  8.0 156.0 %copy-start.4 = (f32[8,512]{1,0:T(8,128)S(1)}, f32[8,512]{1,0:T(8,128)}, u32[]{:S(2)}) copy-start(f32[8,512]{1,0:T(8,128)} %param.11) | copy-start | bytes 49156
  8.0 156.0 %copy-start.5 = (f32[8,512]{1,0:T(8,128)S(1)}, f32[8,512]{1,0:T(8,128)}, u32[]{:S(2)}) copy-start(f32[8,512]{1,0:T(8,128)} %param.10) | copy-start | bytes 49156
  8.0 156.0 %reduce-scatter.2.cloned.1.call-start = ((), (), s32[]{:S(2)}) async-start(), calls=%async_computation.2 | async-start | bytes 270336 | tf_op jit(solution)/shard_map/reduce_scatter | solution.py:14
  8.8 219.2 %all-gather.7.cloned.1.call-start = ((), (), s32[]{:S(2)}) async-start(), calls=%async_computation.4 | async-start | bytes 2228224 | tf_op jit(solution)/shard_map/all_gather | solution.py:23
  9.3 221.7 %all-gather.5.cloned.1.call-start = ((), (), s32[]{:S(2)}) async-start(), calls=%async_computation.3 | async-start | bytes 4456448 | tf_op jit(solution)/shard_map/all_gather | solution.py:28
  12.2 218.9 %copy-start.1 = (bf16[1,128,4096]{2,1,0:T(8,128)(2,1)S(1)}, bf16[1,128,4096]{2,1,0:T(8,128)(2,1)}, u32[]{:S(2)}) copy-start(bf16[1,128,4096]{2,1,0:T(8,128)(2,1)} %param.6) | copy-start | bytes 3145732
  12.2 215.2 %all-to-all-start = ((bf16[128,16,256]{0,2,1:T(8,128)(2,1)}), bf16[128,16,256]{0,2,1:T(8,128)(2,1)S(1)}, u32[]{:S(2)}, u32[]{:S(2)}) async-start(bf16[128,16,256]{0,2,1:T(8,128)(2,1)} %bitcast.5), calls=%async_computation | async-start | bytes 2097152 | tf_op jit(solution)/shard_map/all_to_all | solution.py:22
  228.0 6.8 %copy-start.2 = (bf16[1,128,512]{2,1,0:T(8,128)(2,1)S(1)}, bf16[1,128,512]{2,1,0:T(8,128)(2,1)}, u32[]{:S(2)}) copy-start(bf16[1,128,512]{2,1,0:T(8,128)(2,1)} %param.8) | copy-start | bytes 393220
  231.1 3.7 %copy-start = (bf16[1,4096,512]{2,1,0:T(8,128)(2,1)S(1)}, bf16[1,4096,512]{2,1,0:T(8,128)(2,1)}, u32[]{:S(2)}) copy-start(bf16[1,4096,512]{2,1,0:T(8,128)(2,1)} %all-gather.5.cloned.1.call-done) | copy-start | bytes 12582916
Sparse Core Ops, SparseCore 0:
  11.6 152.3 reduce-scatter.1
Sparse Core Ops, SparseCore 1:
  12.5 65.7 all-gather.6
  81.4 71.1 all-gather.4
where the time goes:
time: 246 us; the launch traced here: 245 us
  waiting for transfers between devices  144 us (59%)
  blocking collectives  62.1 us (25%)
  between operations  15.5 us (6%)
  starting transfers between devices  9.41 us (4%)
  matrix products  9.23 us (4%)
  local copies, waits for them, and re-layouts  3.52 us (1%)
    reduce_scatter x1, waiting for transfers between devices, on_device(): lax.psum_scatter(weight.astype(jnp.float32).astype(jnp.bfloat16), 'replic...  143 us
    all_gather x1, blocking collectives, on_device(): lax.all_gather(global_new.astype(jnp.bfloat16), 'replica', axis=0, tiled=...  62.1 us
    all_to_all x1, starting transfers between devices, on_device(): lax.all_to_all(inputs, 'fsdp', split_axis=1, concat_axis=0, tiled=True)  9.29 us
  transfers between devices with their start and end apart: 4, of which 1 were waited for; matrix products, arithmetic and copies ran while one was open for 3% of the time, Pallas kernels for 0%

commit v1 on v0

--- a/solution.py
+++ b/solution.py
@@ -4,6 +4,11 @@
 from jax.sharding import PartitionSpec as P
 
 D_WIN = 4096
+
+
+def exchange_gather(x, axis, dim):
+    outgoing = jnp.stack([x] * lax.axis_size(axis))
+    return jnp.concatenate(lax.all_to_all(outgoing, axis, 0, 0), axis=dim)
 
 
 def on_device(tokens, local_weight, key_cot, global_weight, momentum, anchor):
@@ -18,7 +23,7 @@
     push = pseudo + 0.1 * (global_weight - anchor)
     momentum_new = 0.9 * momentum + push
     global_new = global_weight - 0.7 * (push + 0.9 * momentum_new)
-    synced = lax.all_gather(global_new.astype(jnp.bfloat16), "replica", axis=0, tiled=True)
+    synced = exchange_gather(global_new.astype(jnp.bfloat16), "replica", 0)
     columns_all = lax.all_to_all(inputs, "fsdp", split_axis=1, concat_axis=0, tiled=True)
     cot_all = lax.all_gather(cot, "fsdp", axis=0, tiled=True)
     wgrad = lax.dot_general(

time: 246 us -> 211 us (0.86)
  the two profiles are of different devices: /device:TPU:16 before, /device:TPU:4 now
where the time goes in v1:
time: 211 us; the launch traced here: 210 us
  waiting for transfers between devices  159 us (75%)
  starting transfers between devices  20.7 us (10%)
  between operations  15.5 us (7%)
  matrix products  9.23 us (4%)
  local copies, waits for them, and re-layouts  4.24 us (2%)
    reduce_scatter x1, waiting for transfers between devices, on_device(): lax.psum_scatter(weight.astype(jnp.float32).astype(jnp.bfloat16), 'replic...  140 us
    all_to_all x1, waiting for transfers between devices, exchange_gather(): return jnp.concatenate(lax.all_to_all(outgoing, axis, 0, 0), axis=dim)  17.2 us
    all_to_all x1, starting transfers between devices, exchange_gather(): return jnp.concatenate(lax.all_to_all(outgoing, axis, 0, 0), axis=dim)  11.1 us
    all_to_all x1, starting transfers between devices, on_device(): lax.all_to_all(inputs, 'fsdp', split_axis=1, concat_axis=0, tiled=True)  9.5 us
  transfers between devices with their start and end apart: 5, of which 2 were waited for; matrix products, arithmetic and copies ran while one was open for 4% of the time, Pallas kernels for 0%

profile of v1, /device:TPU:4, one launch (start us, length us, event | category | flops | bytes accessed | tf_op | source)
XLA Modules:
  0.0 210.3 jit_solution(3086566996455828983)
XLA Ops:
  8.0 0.0 copy-start.3
  8.0 0.0 copy-start.4
  8.0 0.0 copy-start.5
  8.0 0.0 reduce-scatter.2.cloned.1.call-start
  8.1 0.7 reduce-scatter.2.cloned.1.call-update
  8.8 0.0 all-gather.7.cloned.1.call-start
  8.8 0.5 all-gather.7.cloned.1.call-update
  9.3 0.0 all-gather.5.cloned.1.call-start
  9.4 0.5 all-gather.5.cloned.1.call-update
  9.9 2.3 %copy.12 = bf16[1,128,4096]{1,2,0:T(8,128)(2,1)} copy(bf16[1,128,4096]{2,1,0:T(8,128)(2,1)} %param.6) | data formatting | bytes 2097152 | tf_op args[0]
  12.2 9.5 %all-to-all-start = ((bf16[128,16,256]{0,2,1:T(8,128)(2,1)}), bf16[128,16,256]{0,2,1:T(8,128)(2,1)S(1)}, u32[]{:S(2)}, u32[]{:S(2)}) async-start(bf16[128,16,256]{0,2,1:T(8,128)(2,1)} %bitcast.5), calls=%async_computation | async-start | bytes 2097152 | tf_op jit(solution)/shard_map/all_to_all | solution.py:27
  21.7 140.2 %reduce-scatter.2.cloned.1.call-done = bf16[8,512]{1,0:T(8,128)(2,1)} async-done(((bf16[256,512]{1,0:T(8,128)(2,1)}), bf16[8,512]{1,0:T(8,128)(2,1)}) %reduce-scatter.2.cloned.1.call-update) | async-done | bytes 8208 | tf_op jit(solution)/shard_map/reduce_scatter | solution.py:19
  161.9 0.0 copy-done.5
  161.9 1.3 fusion.27
  163.3 0.0 all-to-all-done
  163.3 0.7 stack.2
  164.0 11.1 %all-to-all-start.1 = ((bf16[32,8,512]{2,1,0:T(8,128)(2,1)}), bf16[32,8,512]{2,1,0:T(8,128)(2,1)S(1)}, u32[]{:S(2)}, u32[]{:S(2)}) async-start(bf16[32,8,512]{2,1,0:T(8,128)(2,1)} %stack.2), calls=%async_computation.2 | async-start | bytes 524288 | tf_op jit(solution)/shard_map/all_to_all | solution.py:11
  175.1 0.5 copy.13
  175.7 17.2 %all-to-all-done.1 = bf16[32,8,512]{2,1,0:T(8,128)(2,1)S(1)} async-done(((bf16[32,8,512]{2,1,0:T(8,128)(2,1)}), bf16[32,8,512]{2,1,0:T(8,128)(2,1)S(1)}, u32[]{:S(2)}, u32[]{:S(2)}) %all-to-all-start.1) | async-done | bytes 262176 | tf_op jit(solution)/shard_map/all_to_all | solution.py:11
  192.9 3.1 %fusion.13 = bf16[1,256,512]{2,1,0:T(8,128)(2,1)} fusion(bf16[2048,256]{1,0:T(8,128)(2,1)S(1)} %bitcast.39, bf16[1,2048,512]{2,1,0:T(8,128)(2,1)} %all-gather.7.cloned.1.call-done), kind=kOutput, calls=%fused_computation.10 | convolution fusion | flops 537133056 | bytes 3407872 | tf_op jit(solution)/shard_map/dot_general | solution.py:29
  195.9 3.7 %fusion.22 = bf16[1,128,512]{2,1,0:T(8,128)(2,1)} fusion(bf16[1,4096,512]{2,1,0:T(8,128)(2,1)} %all-gather.5.cloned.1.call-done, bf16[1,128,4096]{2,1,0:T(8,128)(2,1)S(1)} %copy-done.1), kind=kOutput, calls=%fused_computation.13 | convolution fusion | flops 537001984 | bytes 5373952 | tf_op jit(solution)/shard_map/dot_general | solution.py:34
  199.7 0.0 copy-done
  199.7 2.5 %fusion.1 = bf16[1,128,4096]{2,1,0:T(8,128)(2,1)} fusion(bf16[1,4096,512]{2,1,0:T(8,128)(2,1)S(1)} %copy-done, bf16[1,128,512]{2,1,0:T(8,128)(2,1)S(1)} %copy-done.2), kind=kOutput, calls=%fused_computation.2 | convolution fusion | flops 537919488 | bytes 5373952 | tf_op jit(solution)/shard_map/dot_general | solution.py:35
  202.1 0.7 copy.15
  (9 shorter events, 0.0 us)
Async XLA Ops:
  8.0 153.9 %copy-start.3 = (f32[8,512]{1,0:T(8,128)S(1)}, f32[8,512]{1,0:T(8,128)}, u32[]{:S(2)}) copy-start(f32[8,512]{1,0:T(8,128)} %param.9) | copy-start | bytes 49156
  8.0 153.9 %copy-start.4 = (f32[8,512]{1,0:T(8,128)S(1)}, f32[8,512]{1,0:T(8,128)}, u32[]{:S(2)}) copy-start(f32[8,512]{1,0:T(8,128)} %param.11) | copy-start | bytes 49156
  8.0 153.9 %copy-start.5 = (f32[8,512]{1,0:T(8,128)S(1)}, f32[8,512]{1,0:T(8,128)}, u32[]{:S(2)}) copy-start(f32[8,512]{1,0:T(8,128)} %param.10) | copy-start | bytes 49156
  8.0 153.9 %reduce-scatter.2.cloned.1.call-start = ((), (), s32[]{:S(2)}) async-start(), calls=%async_computation.3 | async-start | bytes 270336 | tf_op jit(solution)/shard_map/reduce_scatter | solution.py:19
  8.8 184.1 %all-gather.7.cloned.1.call-start = ((), (), s32[]{:S(2)}) async-start(), calls=%async_computation.5 | async-start | bytes 2228224 | tf_op jit(solution)/shard_map/all_gather | solution.py:28
  9.3 186.6 %all-gather.5.cloned.1.call-start = ((), (), s32[]{:S(2)}) async-start(), calls=%async_computation.4 | async-start | bytes 4456448 | tf_op jit(solution)/shard_map/all_gather | solution.py:33
  12.2 183.7 %copy-start.1 = (bf16[1,128,4096]{2,1,0:T(8,128)(2,1)S(1)}, bf16[1,128,4096]{2,1,0:T(8,128)(2,1)}, u32[]{:S(2)}) copy-start(bf16[1,128,4096]{2,1,0:T(8,128)(2,1)} %param.6) | copy-start | bytes 3145732
  12.2 151.1 %all-to-all-start = ((bf16[128,16,256]{0,2,1:T(8,128)(2,1)}), bf16[128,16,256]{0,2,1:T(8,128)(2,1)S(1)}, u32[]{:S(2)}, u32[]{:S(2)}) async-start(bf16[128,16,256]{0,2,1:T(8,128)(2,1)} %bitcast.5), calls=%async_computation | async-start | bytes 2097152 | tf_op jit(solution)/shard_map/all_to_all | solution.py:27
  164.0 28.9 %all-to-all-start.1 = ((bf16[32,8,512]{2,1,0:T(8,128)(2,1)}), bf16[32,8,512]{2,1,0:T(8,128)(2,1)S(1)}, u32[]{:S(2)}, u32[]{:S(2)}) async-start(bf16[32,8,512]{2,1,0:T(8,128)(2,1)} %stack.2), calls=%async_computation.2 | async-start | bytes 524288 | tf_op jit(solution)/shard_map/all_to_all | solution.py:11
  192.9 6.8 %copy-start.2 = (bf16[1,128,512]{2,1,0:T(8,128)(2,1)S(1)}, bf16[1,128,512]{2,1,0:T(8,128)(2,1)}, u32[]{:S(2)}) copy-start(bf16[1,128,512]{2,1,0:T(8,128)(2,1)} %param.8) | copy-start | bytes 393220
  195.9 3.7 %copy-start = (bf16[1,4096,512]{2,1,0:T(8,128)(2,1)S(1)}, bf16[1,4096,512]{2,1,0:T(8,128)(2,1)}, u32[]{:S(2)}) copy-start(bf16[1,4096,512]{2,1,0:T(8,128)(2,1)} %all-gather.5.cloned.1.call-done) | copy-start | bytes 12582916
Sparse Core Ops, SparseCore 0:
  11.6 150.2 reduce-scatter.1
Sparse Core Ops, SparseCore 1:
  12.5 66.8 all-gather.6
  82.5 70.7 all-gather.4
